TPU v7x, 32 devices: a whole 2x2x4 slice. The times are simulated.
32 devices in a mesh: video: 2 (over x), seq: 8 (over z, y), head: 2 (over core).
Axes of the slice: x: 2, y: 2, z: 4, core: 2. Of those that a mesh axis runs over, the one named last changes fastest.
Arguments:
- query: bfloat16 [6144, 1536], P(('video', 'seq'), 'head'), parts along dimension 0, may hold values from -5 to 5
- key: bfloat16 [6144, 1536], P(('video', 'seq'), 'head'), parts along dimension 0, may hold values from -5 to 5
- value: bfloat16 [6144, 1536], P(('video', 'seq'), 'head'), parts along dimension 0, may hold values from -6 to 6
- stream: bfloat16 [6144, 3072], P(('video', 'seq'), 'head'), parts along dimension 0, may hold values from -12 to 12
- shift_mod: float32 [6144], P('video'), parts along dimension 0, may hold values from -3 to 3
- scale_mod: float32 [6144], P('video'), parts along dimension 0, may hold values from -3 to 3
- out_weight: bfloat16 [1536, 3072], P('seq', 'head'), may hold values from -0.5 to 0.5
Outputs:
- normed: bfloat16 [6144, 3072], P(('video', 'seq'), 'head'), parts along dimension 0
- stream_out: bfloat16 [6144, 3072], P(('video', 'seq'), 'head'), parts along dimension 0
There are 2 independent parts, one for each index of `video`. A program takes and returns all parts, laid end to end along the dimension named above; an argument that names none is the same for every part. Nothing has to cross between parts.
All inputs are finite; a program needn't handle non-finite values.
Results may differ from a plain program's by a relative error of at most 0.0051.
Values may be sent and summed in bfloat16 or wider, within the bound.
A program may use at most 128 MiB of HBM per device.

v0:
```python
import math

import jax
import jax.numpy as jnp
from jax import lax
from jax.sharding import PartitionSpec as P

D = 3072
HD = 128
TILE = 128
HT = 4


def shifted(value, axis, steps):
    count = lax.axis_size(axis)
    leading, last = (max(0, -steps), min(count, count - steps))
    return lax.ppermute(value, axis, [(source, source + steps) for source in range(leading, last)])


def attend_tile(query_tile, keys_all, values_all, visible):
    tile_rows, features = query_tile.shape
    heads_here = features // HD

    def one_head(head):
        head_query = lax.dynamic_slice_in_dim(query_tile, head * HD, HD, 1)
        head_key = lax.dynamic_slice_in_dim(keys_all, head * HD, HD, 1)
        head_value = lax.dynamic_slice_in_dim(values_all, head * HD, HD, 1)
        scores = jnp.einsum(
            "nd,md->nm", head_query, head_key, preferred_element_type=jnp.float32
        ) / math.sqrt(HD)
        scores = jnp.where(visible[None, :], scores, -jnp.inf)
        top = jnp.max(scores, axis=1, keepdims=True)
        expo = jnp.exp(scores - top)
        total = jnp.sum(expo, axis=1, keepdims=True)
        probs = expo.astype(jnp.bfloat16)
        weighted = jnp.dot(probs, head_value, preferred_element_type=jnp.float32)
        return (weighted / total).astype(jnp.bfloat16)

    per_head = lax.map(one_head, jnp.arange(heads_here, dtype=jnp.int32))
    return jnp.transpose(per_head, (1, 0, 2)).reshape(tile_rows, features)


def on_device(query, key, value, stream, shift_mod, scale_mod, out_weight):
    slab_rows = query.shape[0]
    width_tiles = slab_rows // TILE
    layers = lax.axis_size("seq") // HT
    position = lax.axis_index("seq")
    time_tile = position // HT
    height_tile = position % HT
    key_value = jnp.stack([key, value])
    blocks = {}
    vertical = {0: key_value}
    for offset in (HT, -HT):
        vertical[-offset // HT] = shifted(key_value, "seq", offset)
    column = jnp.stack([vertical[-1], vertical[0], vertical[1]])
    sideways = {0: column}
    for offset in (1, -1):
        sideways[-offset] = shifted(column, "seq", offset)
    for across in (-1, 0, 1):
        for upward in (-1, 0, 1):
            blocks[across, upward] = sideways[upward][across + 1]
    neighbours = []
    for across in (-1, 0, 1):
        for upward in (-1, 0, 1):
            inside = (time_tile + across >= 0) & (time_tile + across < layers)
            inside = inside & (height_tile + upward >= 0) & (height_tile + upward < HT)
            neighbours.append((blocks[across, upward], inside))
    results = []
    for tile_pos in range(width_tiles):
        lowest = max(tile_pos - 1, 0)
        highest = min(tile_pos + 1, width_tiles - 1)
        begin = lowest * TILE
        count = (highest - lowest + 1) * TILE
        keys_here = jnp.concatenate(
            [paired[0][begin : begin + count] for paired, inside in neighbours], 0
        )
        values_here = jnp.concatenate(
            [paired[1][begin : begin + count] for paired, inside in neighbours], 0
        )
        flags = jnp.concatenate(
            [jnp.broadcast_to(inside, (count,)) for paired, inside in neighbours]
        )
        query_tile = query[tile_pos * TILE : (tile_pos + 1) * TILE]
        results.append(attend_tile(query_tile, keys_here, values_here, flags))
    attended = jnp.concatenate(results, 0)
    width_cols = D // lax.axis_size("head")
    first_col = lax.axis_index("head") * width_cols
    weight_cols = lax.all_gather(out_weight, "seq", axis=0, tiled=True)
    weight_rows = lax.all_to_all(weight_cols, "head", split_axis=0, concat_axis=1, tiled=True)
    partial_value = jnp.dot(attended, weight_rows, preferred_element_type=jnp.float32)
    share = lax.psum_scatter(partial_value, "head", scatter_dimension=1, tiled=True)
    mixed = stream.astype(jnp.float32) + share
    totals, squares = lax.psum((jnp.sum(mixed, axis=1), jnp.sum(mixed * mixed, axis=1)), "head")
    mean = (totals / D)[:, None]
    var = (squares / D)[:, None] - mean * mean
    scale_part = lax.dynamic_slice_in_dim(scale_mod, first_col, width_cols, 0)
    shift_part = lax.dynamic_slice_in_dim(shift_mod, first_col, width_cols, 0)
    normed = ((mixed - mean) * lax.rsqrt(var + 1e-06) * (1.0 + scale_part) + shift_part).astype(
        jnp.bfloat16
    )
    return (normed, mixed.astype(jnp.bfloat16))


def solution(mesh):
    return jax.shard_map(
        on_device,
        mesh=mesh,
        in_specs=(
            P(("video", "seq"), "head"),
            P(("video", "seq"), "head"),
            P(("video", "seq"), "head"),
            P(("video", "seq"), "head"),
            P("video"),
            P("video"),
            P("seq", "head"),
        ),
        out_specs=(P(("video", "seq"), "head"), P(("video", "seq"), "head")),
        check_vma=False,
    )
```

profile of v0, /device:TPU:27, one launch (start us, length us, event | category | flops | bytes accessed | tf_op | source)
XLA Modules:
  0.0 439.2 jit_solution(9544043463782525171)
XLA Ops:
  8.6 2.0 collective-permute-start.1
  12.0 23.3 %collective-permute-done.1 = bf16[2,384,768]{2,1,0:T(8,128)(2,1)S(1)} collective-permute-done((bf16[2,384,768]{2,1,0:T(8,128)(2,1)S(1)}, bf16[2,384,768]{2,1,0:T(8,128)(2,1)S(1)}, u32[]{:S(2)}, u32[]{:S(2)}) %collective-permute-start.1) | collective-permute-done | bytes 1179680 | tf_op jit(solution)/shard_map/ppermute | solution.py:17
  35.3 31.2 %collective-permute-done = bf16[2,384,768]{2,1,0:T(8,128)(2,1)S(1)} collective-permute-done((bf16[2,384,768]{2,1,0:T(8,128)(2,1)S(1)}, bf16[2,384,768]{2,1,0:T(8,128)(2,1)S(1)}, u32[]{:S(2)}, u32[]{:S(2)}) %collective-permute-start) | collective-permute-done | bytes 1179680 | tf_op jit(solution)/shard_map/ppermute | solution.py:17
  66.5 2.1 pad_maximum_fusion
  68.7 3.1 collective-permute-start.2
  71.8 3.0 collective-permute-start.3
  79.1 2.0 fusion.97
  81.1 79.4 %collective-permute-done.2 = bf16[3,2,384,768]{3,2,1,0:T(8,128)(2,1)} collective-permute-done((bf16[3,2,384,768]{3,2,1,0:T(8,128)(2,1)}, bf16[3,2,384,768]{3,2,1,0:T(8,128)(2,1)}, u32[]{:S(2)}, u32[]{:S(2)}) %collective-permute-start.2) | collective-permute-done | bytes 3538976 | tf_op jit(solution)/shard_map/ppermute | solution.py:17
  162.1 95.5 %collective-permute-done.3 = bf16[3,2,384,768]{3,2,1,0:T(8,128)(2,1)S(1)} collective-permute-done((bf16[3,2,384,768]{3,2,1,0:T(8,128)(2,1)}, bf16[3,2,384,768]{3,2,1,0:T(8,128)(2,1)S(1)}, u32[]{:S(2)}, u32[]{:S(2)}) %collective-permute-start.3) | collective-permute-done | bytes 3538976 | tf_op jit(solution)/shard_map/ppermute | solution.py:17
  257.7 1.5 fusion.78
  259.4 1.5 fusion.76
  266.4 48.3 %while.30 = (s32[]{:T(128)}, bf16[6,128,128]{1,2,0:T(8,128)(2,1)}, pred[2304]{0:T(1024)(128)(4,1)S(1)}, s32[6]{0:T(128)S(1)}, bf16[128,768]{1,0:T(8,128)(2,1)}, ...) while((s32[]{:T(128)}, bf16[6,128,128]{1,2,0:T(8,128)(2,1)}, ...), condition=%wide.region_3.4_spmd, body=%wide.region_0.3_spmd.sunk | while | flops 153091840 | bytes 4921771 | solution.py:39
  267.7 1.5 fusion.116
  269.6 2.1 fusion.118
  271.6 1.5 copy.25
  275.8 1.5 fusion.116
  277.6 2.1 fusion.118
  279.7 1.5 copy.25
  283.9 1.5 fusion.116
  285.7 2.1 fusion.118
  287.7 1.5 copy.25
  291.9 1.5 fusion.116
  293.7 2.1 fusion.118
  295.8 1.5 copy.25
  299.9 1.5 fusion.116
  301.8 2.1 fusion.118
  303.8 1.5 copy.25
  308.0 1.5 fusion.116
  309.8 2.1 fusion.118
  311.9 1.5 copy.25
  320.7 2.4 copy-done.10
  323.1 2.4 copy-done.11
  325.5 28.1 %while.32 = (s32[]{:T(128)}, bf16[6,128,128]{1,2,0:T(8,128)(2,1)S(1)}, pred[2304]{0:T(1024)(128)(4,1)S(1)}, s32[6]{0:T(128)S(1)}, bf16[128,768]{1,0:T(8,128)(2,1...) while((s32[]{:T(128)}, ...), condition=%wide.region_11.12_spmd, body=%wide.region_8.11_spmd.sunk | while | flops 153091840 | bytes 4921263 | solution.py:39
  326.8 1.5 fusion.126
  328.6 1.5 fusion.128
  331.5 1.5 fusion.126
  333.3 1.5 fusion.128
  336.1 1.5 fusion.126
  338.0 1.5 fusion.128
  340.8 1.5 fusion.126
  342.6 1.5 fusion.128
  345.5 1.5 fusion.126
  347.3 1.5 fusion.128
  350.2 1.5 fusion.126
  353.7 30.6 %while.31 = (s32[]{:T(128)}, bf16[6,128,128]{1,2,0:T(8,128)(2,1)S(1)}, pred[3456]{0:T(1024)(128)(4,1)S(1)}, s32[6]{0:T(128)S(1)}, bf16[128,768]{1,0:T(8,128)(2,1...) while((s32[]{:T(128)}, ...), condition=%wide.region_7.8_spmd, body=%wide.region_4.7_spmd.sunk | while | flops 229621504 | bytes 7281711 | solution.py:39
  354.9 1.7 fusion.121
  357.0 1.6 fusion.123
  360.0 1.7 fusion.121
  362.1 1.6 fusion.123
  365.1 1.7 fusion.121
  367.2 1.6 fusion.123
  370.2 1.7 fusion.121
  372.3 1.6 fusion.123
  375.3 1.7 fusion.121
  377.4 1.6 fusion.123
  380.4 1.7 fusion.121
  382.5 1.6 fusion.123
  384.3 12.9 %all_to_all.19 = bf16[2,768,1536]{2,1,0:T(8,128)(2,1)} all-to-all(bf16[2,768,1536]{2,1,0:T(8,128)(2,1)} %bitcast.237), channel_id=1, replica_groups=mesh['video'=2,'seq'=8,'head'=2] {'head'}, dimensions={0} | all-to-all | bytes 9437184 | tf_op jit(solution)/shard_map/all_to_all | solution.py:89
  397.3 6.7 %copy.15 = bf16[768,2,1536]{0,2,1:T(8,128)(2,1)} copy(bf16[768,2,1536]{2,0,1:T(8,128)(2,1)} %bitcast.232) | data formatting | bytes 9437184 | tf_op jit(solution)/shard_map/all_to_all | solution.py:89
  403.9 6.6 %fusion.52 = f32[384,3072]{1,0:T(8,128)} fusion(bf16[768,3072]{0,1:T(8,128)(2,1)} %bitcast.238, bf16[128,768]{0,1:T(8,128)(2,1)S(1)} %bitcast.241, bf16[128,768]{0,1:T(8,128)(2,1)S(1)} %bitcast.239, bf16[128,768]{0,1:T(8,128)(2,1)S(1)} %bitcast.240), kind=kOutput, calls=%fused_computation.82 | convolution fusion | flops 1813708800 | bytes 10027008 | tf_op jit(solution)/shard_map/dot_general | solution.py:90
  411.4 12.3 %reduce-scatter.2.cloned.1.call-done = f32[384,1536]{1,0:T(8,128)} async-done(((f32[384,3072]{1,0:T(8,128)}), f32[384,1536]{1,0:T(8,128)}) %reduce-scatter.2.cloned.1.call-update) | async-done | bytes 2359312 | tf_op jit(solution)/shard_map/reduce_scatter | solution.py:91
  423.7 2.9 fusion.91
  426.5 3.2 all-reduce
  430.4 2.0 fusion.90
  (173 shorter events, 50.1 us)
Async XLA Ops:
  7.2 377.2 %all-gather.2.cloned.1.call-start = ((), (), s32[]{:S(2)}) async-start(), calls=%async_computation.2 | async-start | bytes 5308416 | tf_op jit(solution)/shard_map/all_gather | solution.py:88
  8.6 26.7 %collective-permute-start.1 = (bf16[2,384,768]{2,1,0:T(8,128)(2,1)S(1)}, bf16[2,384,768]{2,1,0:T(8,128)(2,1)S(1)}, u32[]{:S(2)}, u32[]{:S(2)}) collective-permute-start(bf16[2,384,768]{2,1,0:T(8,128)(2,1)S(1)} %get-tuple-element.219), channel_id=1, source_target_pairs={{8,0},{10,2},{12,4},{14,6},{9,1},{11,3},{13,5},{15,7},{24,16},{26,... | collective-permute-start | bytes 3538952 | tf_op jit(solution)/shard_map/ppermute | solution.py:17
  10.7 55.8 %collective-permute-start = (bf16[2,384,768]{2,1,0:T(8,128)(2,1)S(1)}, bf16[2,384,768]{2,1,0:T(8,128)(2,1)S(1)}, u32[]{:S(2)}, u32[]{:S(2)}) collective-permute-start(bf16[2,384,768]{2,1,0:T(8,128)(2,1)S(1)} %get-tuple-element.219), channel_id=1, source_target_pairs={{0,8},{2,10},{4,12},{6,14},{1,9},{3,11},{5,13},{7,15},{16,24},{18,... | collective-permute-start | bytes 3538952 | tf_op jit(solution)/shard_map/ppermute | solution.py:17
  35.3 33.3 %copy-start = (bf16[2,384,768]{2,1,0:T(8,128)(2,1)}, bf16[2,384,768]{2,1,0:T(8,128)(2,1)S(1)}, u32[]{:S(2)}) copy-start(bf16[2,384,768]{2,1,0:T(8,128)(2,1)S(1)} %collective-permute-done.1) | copy-start | bytes 3538948
  66.5 2.2 copy-start.3
  68.7 91.8 %collective-permute-start.2 = (bf16[3,2,384,768]{3,2,1,0:T(8,128)(2,1)}, bf16[3,2,384,768]{3,2,1,0:T(8,128)(2,1)}, u32[]{:S(2)}, u32[]{:S(2)}) collective-permute-start(bf16[3,2,384,768]{3,2,1,0:T(8,128)(2,1)} %pad_maximum_fusion), channel_id=1, source_target_pairs={{0,2},{2,4},{4,6},{6,8},{8,10},{10,12},{12,14},{1,3},{3,5},{5,7},{... | collective-permute-start | bytes 10616840 | tf_op jit(solution)/shard_map/ppermute | solution.py:17
  71.8 185.7 %collective-permute-start.3 = (bf16[3,2,384,768]{3,2,1,0:T(8,128)(2,1)}, bf16[3,2,384,768]{3,2,1,0:T(8,128)(2,1)S(1)}, u32[]{:S(2)}, u32[]{:S(2)}) collective-permute-start(bf16[3,2,384,768]{3,2,1,0:T(8,128)(2,1)} %pad_maximum_fusion), channel_id=1, source_target_pairs={{2,0},{4,2},{6,4},{8,6},{10,8},{12,10},{14,12},{3,1},{5,3},{7,5},{... | collective-permute-start | bytes 10616840 | tf_op jit(solution)/shard_map/ppermute | solution.py:17
  74.9 348.8 %reduce-scatter.2.cloned.1.call-start = ((), (), s32[]{:S(2)}) async-start(), calls=%async_computation.3 | async-start | bytes 7077888 | tf_op jit(solution)/shard_map/reduce_scatter | solution.py:91
  79.0 82.9 %copy-start.4 = (bf16[2,384,768]{2,1,0:T(8,128)(2,1)S(1)}, bf16[2,384,768]{2,1,0:T(8,128)(2,1)}, u32[]{:S(2)}) copy-start(bf16[2,384,768]{2,1,0:T(8,128)(2,1)} %copy-done.3) | copy-start | bytes 3538948
  162.1 97.1 %copy-start.6 = (bf16[384,768]{1,0:T(8,128)(2,1)S(1)}, bf16[384,768]{1,0:T(8,128)(2,1)}, u32[]{:S(2)}) copy-start(bf16[384,768]{1,0:T(8,128)(2,1)} %param.15) | copy-start | bytes 1769476
  162.1 97.1 %copy-start.8 = (bf16[384,768]{1,0:T(8,128)(2,1)S(1)}, bf16[384,768]{1,0:T(8,128)(2,1)}, u32[]{:S(2)}) copy-start(bf16[384,768]{1,0:T(8,128)(2,1)} %param.14) | copy-start | bytes 1769476
  259.3 1.7 copy-start.1
  261.2 1.9 copy-start.13
  261.2 3.0 copy-start.16
  261.2 4.2 copy-start.14
  261.3 5.2 %copy-start.15 = (bf16[2304,768]{1,0:T(8,128)(2,1)}, bf16[2304,768]{1,0:T(8,128)(2,1)S(1)}, u32[]{:S(2)}) copy-start(bf16[2304,768]{1,0:T(8,128)(2,1)S(1)} %get-tuple-element.379) | copy-start | bytes 10616836
  316.1 2.9 copy-start.7
  316.1 2.9 copy-start.9
  318.9 1.6 copy-start.2
  320.7 2.4 copy-start.10
  323.1 2.4 copy-start.11
  397.2 6.7 %copy-start.17 = (bf16[6,128,128]{1,2,0:T(8,128)(2,1)S(1)}, bf16[6,128,128]{1,2,0:T(8,128)(2,1)}, u32[]{:S(2)}) copy-start(bf16[6,128,128]{1,2,0:T(8,128)(2,1)} %get-tuple-element.113) | copy-start | bytes 589828
  410.5 0.7 copy-start.18
  410.5 0.8 copy-start.19
  410.5 13.1 %copy-start.12 = (bf16[384,1536]{1,0:T(8,128)(2,1)S(1)}, bf16[384,1536]{1,0:T(8,128)(2,1)}, u32[]{:S(2)}) copy-start(bf16[384,1536]{1,0:T(8,128)(2,1)} %param.16) | copy-start | bytes 3538948
  423.7 6.7 %copy-start.5 = (f32[384,1536]{1,0:T(8,128)S(1)}, f32[384,1536]{1,0:T(8,128)}, u32[]{:S(2)}) copy-start(f32[384,1536]{1,0:T(8,128)} %reduce-scatter.2.cloned.1.call-done) | copy-start | bytes 7077892
Sparse Core Ops, SparseCore 0:
  75.0 173.9 all-gather.1
  410.7 12.9 reduce-scatter.1
where the time goes:
time: 443 us; the launch traced here: 439 us
  waiting for transfers between devices  242 us (55%)
  matrix products  65.5 us (15%)
  local copies, waits for them, and re-layouts  64 us (14%)
  blocking collectives  16.1 us (4%)
  other arithmetic  15.4 us (3%)
  between operations  14.5 us (3%)
  loops' own time  12.4 us (3%)
  starting transfers between devices  9.58 us (2%)
    ppermute x4, waiting for transfers between devices, shifted(): lax.ppermute(value, axis, [(source, source + steps) for source in range(l...  229 us
    dot_general x18, matrix products, one_head(): weighted = jnp.dot(probs, head_value, preferred_element_type=jnp.float32)  30.9 us
    dot_general x18, matrix products, one_head(): jnp.einsum('nd,md->nm', head_query, head_key, preferred_element_type=jnp....  28 us
    unnamed x72, local copies, waits for them, and re-layouts  24.6 us
    dynamic_update_slice x36, local copies, waits for them, and re-layouts, attend_tile(): per_head = lax.map(one_head, jnp.arange(heads_here, dtype=jnp.int32))  18.5 us
    all_to_all x1, blocking collectives, on_device(): lax.all_to_all(weight_cols, 'head', split_axis=0, concat_axis=1, tiled=True)  12.9 us
    another operation x3, loops' own time, attend_tile(): per_head = lax.map(one_head, jnp.arange(heads_here, dtype=jnp.int32))  12.4 us
    reduce_scatter x1, waiting for transfers between devices, on_device(): lax.psum_scatter(partial_value, 'head', scatter_dimension=1, tiled=True)  12.3 us
  transfers between devices with their start and end apart: 6, of which 5 were waited for; matrix products, arithmetic and copies ran while one was open for 26% of the time, Pallas kernels for 0%

commit v1 on v0

v1 whole, which is shorter than its diff:
```python
import functools
import math

import jax
import jax.numpy as jnp
from jax import lax
from jax.experimental import pallas as pl
from jax.experimental.pallas import tpu as pltpu
from jax.sharding import PartitionSpec as P

HD = 128
TILE = 128
HT = 4
MESH = pl.DeviceIdType.MESH
F32 = jnp.float32
BF16 = jnp.bfloat16


def attention_kernel(
    layers, spans, chunk, q_ref, k_ref, v_ref, out_ref,
    kbuf, vbuf, q_t, acc, top, total, send_sem, recv_sem, att_send, att_recv,
):
    rows, features = q_ref.shape
    chunks = features // chunk
    heads_chunk = chunk // HD
    width_tiles = rows // TILE
    position = lax.axis_index("seq")
    core = lax.axis_index("head")
    time = position // HT
    height = position % HT
    base = time * HT
    edge = (height == 0) | (height == HT - 1)
    inner = jnp.logical_not(edge)
    partner = base + height + 1 - 2 * (height % 2)
    far = base + (height + 2) % HT
    links = []
    if layers == 2:
        links.append((1, position + HT - 2 * base, True, True))
    elif layers > 2:
        links.append((1, position - HT, time > 0, time < layers - 1))
        links.append((2, position + HT, time < layers - 1, time > 0))

    def guarded(condition, body):
        if condition is True:
            body()
        else:
            pl.when(condition)(body)

    barrier = pltpu.get_barrier_semaphore()

    def greet(device):
        pl.semaphore_signal(barrier, inc=1, device_id=device, device_id_type=MESH)

    greet({"seq": partner})
    greet({"seq": far})
    greet({"head": 1 - core})
    peers = 3
    for _, target, sends, _ in links:
        guarded(sends, lambda target=target: greet({"seq": target}))
        peers = peers + (1 if sends is True else jnp.where(sends, 1, 0))
    pl.semaphore_wait(barrier, peers)

    def cols(c):
        return pl.ds(pl.multiple_of(c * chunk, chunk), chunk)

    def copies(span, hop, c, target):
        pair = []
        for which, (own, buf) in enumerate(((k_ref, kbuf), (v_ref, vbuf))):
            dst = buf.at[span, hop, :, cols(c)]
            if hop == 2:
                src = buf.at[span, 1, :, cols(c)]
            elif hop == 1 and span > 0:
                src = buf.at[span, 0, :, cols(c)]
            else:
                src = own.at[:, cols(c)]
            pair.append(pltpu.make_async_remote_copy(
                src_ref=src, dst_ref=dst,
                send_sem=send_sem.at[which, span, hop, c],
                recv_sem=recv_sem.at[which, span, hop, c],
                device_id={"seq": target}, device_id_type=MESH,
            ))
        return pair

    def start(span, hop, c, target):
        for copy in copies(span, hop, c, target):
            copy.start()

    def arrived(span, hop, c):
        for copy in copies(span, hop, c, partner):
            copy.wait_recv()

    def sent(span, hop, c, target):
        for copy in copies(span, hop, c, target):
            copy.wait_send()

    def first_sends(c, carry):
        for span, target, sends, _ in links:
            guarded(sends, lambda span=span, target=target: start(span, 0, c, target))
        start(0, 1, c, partner)
        return carry

    lax.fori_loop(0, chunks, first_sends, 0)

    for head in range(features // HD):
        q_t[head] = q_ref[:, head * HD : (head + 1) * HD].astype(F32).T.astype(BF16)
    acc[...] = jnp.zeros_like(acc)
    total[...] = jnp.zeros_like(total)
    top[...] = jnp.full_like(top, -jnp.inf)
    factor = math.log2(math.e) / math.sqrt(HD)

    def attend(keys, values, c):
        def one_head(index, carry):
            head = c * heads_chunk + index
            here = pl.ds(pl.multiple_of(head * HD, HD), HD)
            scores = jnp.dot(keys[:, here], q_t[head], preferred_element_type=F32)
            old = top[head]
            parts, news, sums = [], [], []
            for tile in range(width_tiles):
                low = max(tile - 1, 0) * TILE
                high = min(tile + 2, width_tiles) * TILE
                at = slice(tile * TILE, (tile + 1) * TILE)
                seen = scores[low:high, at] * factor
                new = jnp.maximum(jnp.max(seen, axis=0, keepdims=True), old[:, at])
                expo = jnp.exp2(seen - new)
                sums.append(jnp.sum(expo, axis=0, keepdims=True))
                news.append(new)
                column = [expo.astype(BF16)]
                if low > 0:
                    column.insert(0, jnp.zeros((low, TILE), BF16))
                if high < rows:
                    column.append(jnp.zeros((rows - high, TILE), BF16))
                parts.append(jnp.concatenate(column, 0) if len(column) > 1 else column[0])
            probs = jnp.concatenate(parts, 1)
            new = jnp.concatenate(news, 1)
            scale = jnp.exp2(old - new)
            top[head] = new
            total[head] = total[head] * scale + jnp.concatenate(sums, 1)
            weighted = lax.dot_general(
                values[:, here], probs, (((0,), (0,)), ((), ())), preferred_element_type=F32
            )
            acc[head] = acc[head] * scale + weighted
            return carry

        lax.fori_loop(0, heads_chunk, one_head, 0)

    def attend_slot(span, hop, c):
        attend(kbuf.at[span, hop], vbuf.at[span, hop], c)

    def own_block(c, carry):
        attend(k_ref, v_ref, c)
        return carry

    lax.fori_loop(0, chunks, own_block, 0)

    valid = [(0, True)] + [(span, has) for span, _, _, has in links]

    def far_blocks(c):
        for span, has in valid:
            def body(span=span):
                arrived(span, 2, c)
                attend_slot(span, 2, c)
            guarded(inner if has is True else inner & has, body)

    def step(c, carry):
        arrived(0, 1, c)
        pl.when(edge)(lambda: start(0, 2, c, far))
        for span, has in valid[1:]:
            def body(span=span):
                arrived(span, 0, c)
                start(span, 1, c, partner)
            guarded(has, body)
        attend_slot(0, 1, c)
        for span, has in valid[1:]:
            guarded(has, lambda span=span: attend_slot(span, 0, c))
        for span, has in valid[1:]:
            def body(span=span):
                arrived(span, 1, c)
                pl.when(edge)(lambda: start(span, 2, c, far))
                attend_slot(span, 1, c)
            guarded(has, body)
        pl.when(c > 0)(lambda: far_blocks(c - 1))
        return carry

    lax.fori_loop(0, chunks, step, 0)
    far_blocks(chunks - 1)

    for head in range(features // HD):
        done = acc[head] / total[head]
        out_ref[core, :, head * HD : (head + 1) * HD] = done.T.astype(BF16)
    across = pltpu.make_async_remote_copy(
        src_ref=out_ref.at[core], dst_ref=out_ref.at[core],
        send_sem=att_send, recv_sem=att_recv,
        device_id={"head": 1 - core}, device_id_type=MESH,
    )
    across.start()

    def drain(c, carry):
        for span, target, sends, _ in links:
            guarded(sends, lambda span=span, target=target: sent(span, 0, c, target))
        for span, has in valid:
            def body(span=span):
                sent(span, 1, c, partner)
                pl.when(edge)(lambda: sent(span, 2, c, far))
            guarded(has, body)
        return carry

    lax.fori_loop(0, chunks, drain, 0)
    across.wait_send()
    arrive = pltpu.make_async_remote_copy(
        src_ref=out_ref.at[1 - core], dst_ref=out_ref.at[1 - core],
        send_sem=att_send, recv_sem=att_recv,
        device_id={"head": 1 - core}, device_id_type=MESH,
    )
    arrive.wait_recv()


def attention(query, key, value, layers, heads_axis):
    rows, features = query.shape
    heads = features // HD
    chunk = 2 * HD if heads % 2 == 0 else HD
    chunks = features // chunk
    spans = min(layers, 3)
    vmem = pl.BlockSpec(memory_space=pltpu.VMEM)
    return pl.pallas_call(
        functools.partial(attention_kernel, layers, spans, chunk),
        out_shape=jax.ShapeDtypeStruct((heads_axis, rows, features), BF16),
        in_specs=[vmem] * 3,
        out_specs=vmem,
        scratch_shapes=[
            pltpu.VMEM((spans, 3, rows, features), BF16),
            pltpu.VMEM((spans, 3, rows, features), BF16),
            pltpu.VMEM((heads, HD, rows), BF16),
            pltpu.VMEM((heads, HD, rows), F32),
            pltpu.VMEM((heads, 1, rows), F32),
            pltpu.VMEM((heads, 1, rows), F32),
            pltpu.SemaphoreType.DMA((2, spans, 3, chunks)),
            pltpu.SemaphoreType.DMA((2, spans, 3, chunks)),
            pltpu.SemaphoreType.DMA,
            pltpu.SemaphoreType.DMA,
        ],
        compiler_params=pltpu.CompilerParams(
            collective_id=0, has_side_effects=True, vmem_limit_bytes=40 * 1024 * 1024
        ),
        cost_estimate=pl.CostEstimate(
            flops=4 * spans * 3 * rows * rows * features,
            bytes_accessed=100_000_000,
            transcendentals=spans * 3 * rows * rows * heads,
        ),
        name="tile_attention",
    )(query, key, value)


def project_kernel(
    width, att_ref, weight_ref, stream_ref, shift_ref, scale_ref, normed_ref, stream_out_ref,
    mixed, mine, theirs, send_sem, recv_sem,
):
    rows, columns = stream_ref.shape
    parts, _, depth = att_ref.shape
    core = lax.axis_index("head")
    other = {"head": 1 - core}
    barrier = pltpu.get_barrier_semaphore()
    pl.semaphore_signal(barrier, inc=1, device_id=other, device_id_type=MESH)
    step = 2 * HD
    sums = jnp.zeros((rows, HD), F32)
    squares = jnp.zeros((rows, HD), F32)
    for begin in range(0, columns, step):
        at = slice(begin, begin + step)
        block = stream_ref[:, at].astype(F32)
        product = jnp.dot(att_ref[0], weight_ref[0:depth, at], preferred_element_type=F32)
        for part in range(1, parts):
            product += jnp.dot(
                att_ref[part], weight_ref[part * depth : (part + 1) * depth, at],
                preferred_element_type=F32,
            )
        block = block + product
        mixed[:, at] = block
        stream_out_ref[:, at] = block.astype(BF16)
        for inside in range(0, step, HD):
            piece = block[:, inside : inside + HD]
            sums += piece
            squares += piece * piece
    lane = lax.broadcasted_iota(jnp.int32, (rows, HD), 1)
    sum_here = jnp.sum(sums, axis=1, keepdims=True)
    square_here = jnp.sum(squares, axis=1, keepdims=True)
    mine[...] = jnp.where(lane < HD // 2, sum_here, square_here)
    pl.semaphore_wait(barrier, 1)
    copy = pltpu.make_async_remote_copy(
        src_ref=mine, dst_ref=theirs, send_sem=send_sem, recv_sem=recv_sem,
        device_id=other, device_id_type=MESH,
    )
    copy.start()
    copy.wait()
    both = theirs[...]
    mean = (sum_here + both[:, 0:1]) / width
    var = (square_here + both[:, HD - 1 : HD]) / width - mean * mean
    inverse = lax.rsqrt(var + 1e-06)
    for begin in range(0, columns, step):
        at = slice(begin, begin + step)
        here = pl.ds(pl.multiple_of(core * columns + begin, step), step)
        gain = 1.0 + scale_ref[:, here]
        normed_ref[:, at] = (
            (mixed[:, at] - mean) * inverse * gain + shift_ref[:, here]
        ).astype(BF16)


def project(att, weight, stream, shift_mod, scale_mod):
    rows, columns = stream.shape
    width = shift_mod.shape[1]
    vmem = pl.BlockSpec(memory_space=pltpu.VMEM)
    return pl.pallas_call(
        functools.partial(project_kernel, width),
        out_shape=(
            jax.ShapeDtypeStruct((rows, columns), BF16),
            jax.ShapeDtypeStruct((rows, columns), BF16),
        ),
        in_specs=[vmem] * 5,
        out_specs=(vmem, vmem),
        scratch_shapes=[
            pltpu.VMEM((rows, columns), F32),
            pltpu.VMEM((rows, HD), F32),
            pltpu.VMEM((rows, HD), F32),
            pltpu.SemaphoreType.DMA,
            pltpu.SemaphoreType.DMA,
        ],
        compiler_params=pltpu.CompilerParams(
            collective_id=1, has_side_effects=True, vmem_limit_bytes=40 * 1024 * 1024
        ),
        cost_estimate=pl.CostEstimate(
            flops=2 * rows * columns * weight.shape[0],
            bytes_accessed=12_000_000,
            transcendentals=rows,
        ),
        name="project_norm",
    )(att, weight, stream, shift_mod, scale_mod)


def on_device(query, key, value, stream, shift_mod, scale_mod, out_weight):
    layers = lax.axis_size("seq") // HT
    weight = lax.all_gather(out_weight, "seq", axis=0, tiled=True)
    att = attention(query, key, value, layers, lax.axis_size("head"))
    return project(att, weight, stream, shift_mod[None, :], scale_mod[None, :])


def solution(mesh):
    return jax.shard_map(
        on_device,
        mesh=mesh,
        in_specs=(
            P(("video", "seq"), "head"),
            P(("video", "seq"), "head"),
            P(("video", "seq"), "head"),
            P(("video", "seq"), "head"),
            P("video"),
            P("video"),
            P("seq", "head"),
        ),
        out_specs=(P(("video", "seq"), "head"), P(("video", "seq"), "head")),
        check_vma=False,
    )
```

time: 443 us -> 182 us (0.41)
  waiting for transfers between devices: 242 us -> 0.7 us
  Pallas kernels: 0 us -> 158 us
  matrix products: 65.5 us -> 0 us
  local copies, waits for them, and re-layouts: 64 us -> 7.55 us
  blocking collectives: 16.1 us -> 0 us
  other arithmetic: 15.4 us -> 0 us
  loops' own time: 12.4 us -> 0 us
  starting transfers between devices: 9.58 us -> 0.04 us
    ppermute x4 -> x0, waiting for transfers between devices: 229 us -> none  [shifted(): lax.ppermute(value, axis, [(source, source + steps) for source in range(l...]
    pallas_call x0 -> x2, Pallas kernels: none -> 158 us  [the longest x1 154 us: attention(): pl.pallas_call(functools.partial(attention_kernel, layers, spans, chunk),...]
    dot_general x37 -> x0, matrix products: 65.5 us -> none  [the longest x18 30.9 us: one_head(): weighted = jnp.dot(probs, head_value, preferred_element_type=jnp.float32)]
    dynamic_update_slice x36 -> x0, local copies, waits for them, and re-layouts: 18.5 us -> none  [attend_tile(): per_head = lax.map(one_head, jnp.arange(heads_here, dtype=jnp.int32))]
    unnamed x72 -> x16, local copies, waits for them, and re-layouts: 24.6 us -> 7.55 us
    all_to_all x1 -> x0, blocking collectives: 12.9 us -> none  [on_device(): lax.all_to_all(weight_cols, 'head', split_axis=0, concat_axis=1, tiled=True)]
    another operation x3 -> x0, loops' own time: 12.4 us -> none  [attend_tile(): per_head = lax.map(one_head, jnp.arange(heads_here, dtype=jnp.int32))]
    reduce_scatter x1 -> x0, waiting for transfers between devices: 12.3 us -> none  [on_device(): lax.psum_scatter(partial_value, 'head', scatter_dimension=1, tiled=True)]
  transfers between devices with their start and end apart: 6 -> 1, of which waited for: 5 -> 0; matrix products, arithmetic and copies ran while one was open for 26% -> 0% of each run, Pallas kernels for 0% -> 85%
where the time goes in v1:
time: 182 us; the launch traced here: 180 us
  Pallas kernels  158 us (87%)
  between operations  14.1 us (8%)
  local copies, waits for them, and re-layouts  7.55 us (4%)
    pallas_call x1, Pallas kernels, attention(): pl.pallas_call(functools.partial(attention_kernel, layers, spans, chunk),...  154 us
    unnamed x16, local copies, waits for them, and re-layouts  7.55 us
    pallas_call x1, Pallas kernels, project(): pl.pallas_call(functools.partial(project_kernel, width), out_shape=(jax.S...  3.81 us
  transfers between devices with their start and end apart: 1, of which 0 were waited for; matrix products, arithmetic and copies ran while one was open for 0% of the time, Pallas kernels for 85%

profile of v1, /device:TPU:27, one launch (start us, length us, event | category | flops | bytes accessed | tf_op | source)
XLA Modules:
  0.0 179.9 jit_solution(9240714992100159261)
XLA Ops:
  7.2 0.0 all-gather.2.cloned.1.call-start
  7.2 0.7 all-gather.2.cloned.1.call-update
  7.9 0.0 copy-start.4
  7.9 1.1 copy-done.4
  9.0 0.0 copy-start.5
  9.0 1.1 copy-done.5
  10.0 0.0 copy-start.6
  10.0 1.1 copy-done.6
  11.1 0.0 copy-start.1
  11.1 0.0 copy-start.2
  11.1 0.0 copy-start.3
  11.1 153.7 %tile_attention.1.att_ref = bf16[2,384,768]{2,1,0:T(8,128)(2,1)S(1)} custom-call(bf16[384,768]{1,0:T(8,128)(2,1)S(1)} %copy-done.4, bf16[384,768]{1,0:T(8,128)(2,1)S(1)} %copy-done.5, bf16[384,768]{1,0:T(8,128)(2,1)S(1)} %copy-done.6), custom_call_target="tpu_custom_call" | custom-call | flops 2717908992 | bytes 100000000 | tf_op jit(solution)/shard_map/tile_attention/pallas_call | solution.py:224
  164.8 0.0 all-gather.2.cloned.1.call-done.weight_ref
  164.9 0.0 copy-done.1
  164.9 0.0 copy-done.2
  164.9 0.0 copy-done.3
  164.9 0.0 copy-start
  164.9 2.3 %copy-done = bf16[1536,1536]{1,0:T(8,128)(2,1)S(1)} copy-done((bf16[1536,1536]{1,0:T(8,128)(2,1)S(1)}, bf16[1536,1536]{1,0:T(8,128)(2,1)}, u32[]{:S(2)}) %copy-start) | copy-done | bytes 4718616
  167.2 3.8 %project_norm.1 = (bf16[384,1536]{1,0:T(8,128)(2,1)S(1)}, bf16[384,1536]{1,0:T(8,128)(2,1)S(1)}) custom-call(bf16[2,384,768]{2,1,0:T(8,128)(2,1)S(1)} %tile_attention.1.att_ref, bf16[1536,1536]{1,0:T(8,128)(2,1)S(1)} %copy-done, bf16[384,1536]{1,0:T(8,128)(2,1)S(1)} %copy-done.1, f32[1,3072]{1,0:T(1,128)S(1)} %bitcast.2, f32[1,3072]{1,0:T(1,128)S(1)} %bitcast.3), custom_call_target="tpu_custom_call" | custom-call | flops 1811939328 | bytes 12000000 | tf_op jit(solution)/shard_map/project_norm/pallas_call | solution.py:310
  171.0 1.0 copy.11
  172.1 1.0 copy.12
Async XLA Ops:
  7.2 157.7 %all-gather.2.cloned.1.call-start = ((), (), s32[]{:S(2)}) async-start(), calls=%async_computation | async-start | bytes 5308416 | tf_op jit(solution)/shard_map/all_gather | solution.py:339
  7.9 1.1 copy-start.4
  9.0 1.1 copy-start.5
  10.0 1.1 copy-start.6
  11.1 153.8 %copy-start.1 = (bf16[384,1536]{1,0:T(8,128)(2,1)S(1)}, bf16[384,1536]{1,0:T(8,128)(2,1)}, u32[]{:S(2)}) copy-start(bf16[384,1536]{1,0:T(8,128)(2,1)} %stream_ref.1) | copy-start | bytes 3538948
  11.1 153.8 %copy-start.2 = (f32[3072]{0:T(1024)S(1)}, f32[3072]{0:T(1024)}, u32[]{:S(2)}) copy-start(f32[3072]{0:T(1024)} %param.11) | copy-start | bytes 36868
  11.1 153.8 %copy-start.3 = (f32[3072]{0:T(1024)S(1)}, f32[3072]{0:T(1024)}, u32[]{:S(2)}) copy-start(f32[3072]{0:T(1024)} %param.12) | copy-start | bytes 36868
  164.9 2.3 %copy-start = (bf16[1536,1536]{1,0:T(8,128)(2,1)S(1)}, bf16[1536,1536]{1,0:T(8,128)(2,1)}, u32[]{:S(2)}) copy-start(bf16[1536,1536]{1,0:T(8,128)(2,1)} %all-gather.2.cloned.1.call-done.weight_ref) | copy-start | bytes 14155780
Sparse Core Ops, SparseCore 0:
  10.2 131.4 all-gather.1

commit v2 on v1

--- a/solution.py
+++ b/solution.py
@@ -17,8 +17,9 @@
 
 
 def attention_kernel(
-    layers, spans, chunk, q_ref, k_ref, v_ref, out_ref,
+    layers, spans, chunk, ring, videos, q_ref, k_ref, v_ref, w_ref, out_ref, weight_ref,
     kbuf, vbuf, q_t, acc, top, total, send_sem, recv_sem, att_send, att_recv,
+    ring_send, ring_recv, video_send, video_recv,
 ):
     rows, features = q_ref.shape
     chunks = features // chunk
@@ -46,6 +47,72 @@
         else:
             pl.when(condition)(body)
 
+    video = lax.axis_index("video")
+    shard, columns = w_ref.shape
+    piece = columns // videos
+    place = jnp.where(position % 2 == 0, position // 2, ring - 1 - position // 2)
+    reach = ((ring - 1) // 2, ring // 2)
+
+    def ring_device(index):
+        index = (index + ring) % ring
+        return jnp.where(index < ring // 2, 2 * index, 2 * (ring - 1 - index) + 1)
+
+    def piece_cols(of):
+        return pl.ds(pl.multiple_of(of * piece, piece), piece)
+
+    def block(direction, distance, of):
+        owner = ring_device(place - distance if direction == 0 else place + distance)
+        return weight_ref.at[pl.ds(pl.multiple_of(owner * shard, shard), shard), piece_cols(of)]
+
+    def ring_copy(direction, distance, first=False):
+        there = block(direction, distance - 1, video)
+        return pltpu.make_async_remote_copy(
+            src_ref=w_ref.at[:, piece_cols(video)] if first else there, dst_ref=there,
+            send_sem=ring_send.at[direction, distance - 1],
+            recv_sem=ring_recv.at[direction, distance - 1],
+            device_id={"seq": ring_device(place + 1 if direction == 0 else place - 1)},
+            device_id_type=MESH,
+        )
+
+    def video_copy(direction, distance, ahead, of):
+        there = block(direction, distance, of)
+        return pltpu.make_async_remote_copy(
+            src_ref=there, dst_ref=there,
+            send_sem=video_send.at[ahead - 1, direction, distance - 1],
+            recv_sem=video_recv.at[ahead - 1, direction, distance - 1],
+            device_id={"video": lax.rem(video + ahead, videos)}, device_id_type=MESH,
+        )
+
+    def ring_arrived(direction, distance):
+        there = block(direction, distance, video)
+        pltpu.make_async_remote_copy(
+            src_ref=there, dst_ref=there,
+            send_sem=ring_send.at[direction, distance - 1],
+            recv_sem=ring_recv.at[direction, distance - 1],
+            device_id={"seq": ring_device(place + 1)}, device_id_type=MESH,
+        ).wait_recv()
+
+    def weight_step(distance):
+        for direction in (1, 0):
+            def body(direction=direction):
+                ring_arrived(direction, distance)
+                pl.when(distance < reach[direction])(
+                    lambda: ring_copy(direction, distance + 1).start()
+                )
+                for ahead in range(1, videos):
+                    video_copy(direction, distance, ahead, video).start()
+            pl.when(distance <= reach[direction])(body)
+
+    def weight_drain(distance):
+        for direction in (1, 0):
+            def body(direction=direction):
+                ring_copy(direction, distance).wait_send()
+                for ahead in range(1, videos):
+                    source = lax.rem(video + videos - ahead, videos)
+                    video_copy(direction, distance, ahead, video).wait_send()
+                    video_copy(direction, distance, ahead, source).wait_recv()
+            pl.when(distance <= reach[direction])(body)
+
     barrier = pltpu.get_barrier_semaphore()
 
     def greet(device):
@@ -54,7 +121,11 @@
     greet({"seq": partner})
     greet({"seq": far})
     greet({"head": 1 - core})
-    peers = 3
+    greet({"seq": ring_device(place + 1)})
+    greet({"seq": ring_device(place - 1)})
+    for ahead in range(1, videos):
+        greet({"video": lax.rem(video + ahead, videos)})
+    peers = 4 + videos
     for _, target, sends, _ in links:
         guarded(sends, lambda target=target: greet({"seq": target}))
         peers = peers + (1 if sends is True else jnp.where(sends, 1, 0))
@@ -63,13 +134,13 @@
     def cols(c):
         return pl.ds(pl.multiple_of(c * chunk, chunk), chunk)
 
-    def copies(span, hop, c, target):
+    def copies(span, hop, c, target, crossed=False):
         pair = []
         for which, (own, buf) in enumerate(((k_ref, kbuf), (v_ref, vbuf))):
             dst = buf.at[span, hop, :, cols(c)]
             if hop == 2:
-                src = buf.at[span, 1, :, cols(c)]
-            elif hop == 1 and span > 0:
+                src = buf.at[span, 3 if crossed else 1, :, cols(c)]
+            elif span > 0 and hop > 0:
                 src = buf.at[span, 0, :, cols(c)]
             else:
                 src = own.at[:, cols(c)]
@@ -81,9 +152,25 @@
             ))
         return pair
 
-    def start(span, hop, c, target):
-        for copy in copies(span, hop, c, target):
+    def start(span, hop, c, target, crossed=False):
+        for copy in copies(span, hop, c, target, crossed):
             copy.start()
+
+    def is_crossed(c):
+        return c % 3 == 1
+
+    def start_own(span, c):
+        start(span, 1, c, partner)
+        pl.when(inner & is_crossed(c))(lambda: start(span, 3, c, far))
+
+    def pass_straight(span, c):
+        pl.when(edge & jnp.logical_not(is_crossed(c)))(lambda: start(span, 2, c, far))
+
+    def pass_crossed(span, c):
+        def body():
+            arrived(span, 3, c)
+            start(span, 2, c, partner, True)
+        pl.when(edge & is_crossed(c))(body)
 
     def arrived(span, hop, c):
         for copy in copies(span, hop, c, partner):
@@ -96,10 +183,14 @@
     def first_sends(c, carry):
         for span, target, sends, _ in links:
             guarded(sends, lambda span=span, target=target: start(span, 0, c, target))
-        start(0, 1, c, partner)
+        start_own(0, c)
         return carry
 
     lax.fori_loop(0, chunks, first_sends, 0)
+    for direction in (1, 0):
+        if reach[direction] > 0:
+            ring_copy(direction, 1, True).start()
+    weight_ref[pl.ds(pl.multiple_of(position * shard, shard), shard), :] = w_ref[...]
 
     for head in range(features // HD):
         q_t[head] = q_ref[:, head * HD : (head + 1) * HD].astype(F32).T.astype(BF16)
@@ -163,11 +254,12 @@
 
     def step(c, carry):
         arrived(0, 1, c)
-        pl.when(edge)(lambda: start(0, 2, c, far))
+        pass_straight(0, c)
+        pass_crossed(0, c)
         for span, has in valid[1:]:
             def body(span=span):
                 arrived(span, 0, c)
-                start(span, 1, c, partner)
+                start_own(span, c)
             guarded(has, body)
         attend_slot(0, 1, c)
         for span, has in valid[1:]:
@@ -175,13 +267,22 @@
         for span, has in valid[1:]:
             def body(span=span):
                 arrived(span, 1, c)
-                pl.when(edge)(lambda: start(span, 2, c, far))
+                pass_straight(span, c)
+                pass_crossed(span, c)
                 attend_slot(span, 1, c)
             guarded(has, body)
         pl.when(c > 0)(lambda: far_blocks(c - 1))
+        pl.when(c < reach[1])(lambda: weight_step(c + 1))
         return carry
 
     lax.fori_loop(0, chunks, step, 0)
+
+    def late_weights(c, carry):
+        weight_step(c + 1)
+        return carry
+
+    if reach[1] > chunks:
+        lax.fori_loop(chunks, reach[1], late_weights, 0)
     far_blocks(chunks - 1)
 
     for head in range(features // HD):
@@ -201,10 +302,17 @@
             def body(span=span):
                 sent(span, 1, c, partner)
                 pl.when(edge)(lambda: sent(span, 2, c, far))
+                pl.when(inner & is_crossed(c))(lambda: sent(span, 3, c, far))
             guarded(has, body)
         return carry
 
     lax.fori_loop(0, chunks, drain, 0)
+
+    def drain_weights(c, carry):
+        weight_drain(c + 1)
+        return carry
+
+    lax.fori_loop(0, reach[1], drain_weights, 0)
     across.wait_send()
     arrive = pltpu.make_async_remote_copy(
         src_ref=out_ref.at[1 - core], dst_ref=out_ref.at[1 - core],
@@ -214,29 +322,38 @@
     arrive.wait_recv()
 
 
-def attention(query, key, value, layers, heads_axis):
+def attention(query, key, value, out_weight, layers, heads_axis, ring, videos):
     rows, features = query.shape
     heads = features // HD
-    chunk = 2 * HD if heads % 2 == 0 else HD
+    chunk = HD
     chunks = features // chunk
     spans = min(layers, 3)
+    shard, columns = out_weight.shape
+    hops = ring // 2
     vmem = pl.BlockSpec(memory_space=pltpu.VMEM)
     return pl.pallas_call(
-        functools.partial(attention_kernel, layers, spans, chunk),
-        out_shape=jax.ShapeDtypeStruct((heads_axis, rows, features), BF16),
-        in_specs=[vmem] * 3,
-        out_specs=vmem,
+        functools.partial(attention_kernel, layers, spans, chunk, ring, videos),
+        out_shape=(
+            jax.ShapeDtypeStruct((heads_axis, rows, features), BF16),
+            jax.ShapeDtypeStruct((ring * shard, columns), BF16),
+        ),
+        in_specs=[vmem] * 4,
+        out_specs=(vmem, vmem),
         scratch_shapes=[
-            pltpu.VMEM((spans, 3, rows, features), BF16),
-            pltpu.VMEM((spans, 3, rows, features), BF16),
+            pltpu.VMEM((spans, 4, rows, features), BF16),
+            pltpu.VMEM((spans, 4, rows, features), BF16),
             pltpu.VMEM((heads, HD, rows), BF16),
             pltpu.VMEM((heads, HD, rows), F32),
             pltpu.VMEM((heads, 1, rows), F32),
             pltpu.VMEM((heads, 1, rows), F32),
-            pltpu.SemaphoreType.DMA((2, spans, 3, chunks)),
-            pltpu.SemaphoreType.DMA((2, spans, 3, chunks)),
+            pltpu.SemaphoreType.DMA((2, spans, 4, chunks)),
+            pltpu.SemaphoreType.DMA((2, spans, 4, chunks)),
             pltpu.SemaphoreType.DMA,
             pltpu.SemaphoreType.DMA,
+            pltpu.SemaphoreType.DMA((2, hops)),
+            pltpu.SemaphoreType.DMA((2, hops)),
+            pltpu.SemaphoreType.DMA((max(videos - 1, 1), 2, hops)),
+            pltpu.SemaphoreType.DMA((max(videos - 1, 1), 2, hops)),
         ],
         compiler_params=pltpu.CompilerParams(
             collective_id=0, has_side_effects=True, vmem_limit_bytes=40 * 1024 * 1024
@@ -247,7 +364,7 @@
             transcendentals=spans * 3 * rows * rows * heads,
         ),
         name="tile_attention",
-    )(query, key, value)
+    )(query, key, value, out_weight)
 
 
 def project_kernel(
@@ -336,8 +453,10 @@
 
 def on_device(query, key, value, stream, shift_mod, scale_mod, out_weight):
     layers = lax.axis_size("seq") // HT
-    weight = lax.all_gather(out_weight, "seq", axis=0, tiled=True)
-    att = attention(query, key, value, layers, lax.axis_size("head"))
+    att, weight = attention(
+        query, key, value, out_weight, layers,
+        lax.axis_size("head"), lax.axis_size("seq"), lax.axis_size("video"),
+    )
     return project(att, weight, stream, shift_mod[None, :], scale_mod[None, :])
 
 

time: 182 us -> 136 us (0.75)
  Pallas kernels: 158 us -> 127 us
  between operations: 14.1 us -> 0.69 us
    pallas_call x1, Pallas kernels: 154 us -> 123 us  [attention(): pl.pallas_call(functools.partial(attention_kernel, layers, spans, chunk,...]
  transfers between devices with their start and end apart: 1 -> 0, of which waited for: 0 -> 0; matrix products, arithmetic and copies ran while one was open for 0% -> 0% of each run, Pallas kernels for 85% -> 0%
where the time goes in v2:
time: 136 us; the launch traced here: 134 us
  Pallas kernels  127 us (93%)
  local copies, waits for them, and re-layouts  6.29 us (5%)
    pallas_call x1, Pallas kernels, attention(): pl.pallas_call(functools.partial(attention_kernel, layers, spans, chunk,...  123 us
    unnamed x16, local copies, waits for them, and re-layouts  6.29 us
    pallas_call x1, Pallas kernels, project(): pl.pallas_call(functools.partial(project_kernel, width), out_shape=(jax.S...  3.85 us

profile of v2, /device:TPU:27, one launch (start us, length us, event | category | flops | bytes accessed | tf_op | source)
XLA Modules:
  0.0 133.8 jit_solution(1069587607394244615)
XLA Ops:
  0.6 0.0 copy-start.3
  0.6 1.1 copy-done.3
  1.7 0.0 copy-start.4
  1.7 1.1 copy-done.4
  2.8 0.0 copy-start.5
  2.8 1.1 copy-done.5
  3.8 0.0 copy-start.6
  3.8 1.1 copy-done.6
  4.9 0.0 copy-start
  4.9 0.0 copy-start.1
  4.9 0.0 copy-start.2
  4.9 123.0 %tile_attention.1 = (bf16[2,384,768]{2,1,0:T(8,128)(2,1)S(1)}, bf16[1536,1536]{1,0:T(8,128)(2,1)S(1)}) custom-call(bf16[384,768]{1,0:T(8,128)(2,1)S(1)} %copy-done.3, bf16[384,768]{1,0:T(8,128)(2,1)S(1)} %copy-done.4, bf16[384,768]{1,0:T(8,128)(2,1)S(1)} %copy-done.5, bf16[192,1536]{1,0:T(8,128)(2,1)S(1)} %copy-done.6), custom_call_target="tpu_custom_call" | custom-call | flops 2717908992 | bytes 100000000 | tf_op jit(solution)/shard_map/tile_attention/pallas_call | solution.py:334
  127.9 0.0 copy-done
  127.9 0.0 copy-done.1
  127.9 0.0 copy-done.2
  127.9 3.8 %project_norm.1 = (bf16[384,1536]{1,0:T(8,128)(2,1)S(1)}, bf16[384,1536]{1,0:T(8,128)(2,1)S(1)}) custom-call(bf16[2,384,768]{2,1,0:T(8,128)(2,1)S(1)} %get-tuple-element.4.att_ref, bf16[1536,1536]{1,0:T(8,128)(2,1)S(1)} %get-tuple-element.5.weight_ref, bf16[384,1536]{1,0:T(8,128)(2,1)S(1)} %copy-done, f32[1,3072]{1,0:T(1,128)S(1)} %bitcast.2, ...), custom_call_target="tpu_custom_call" | custom-call | flops 1811939328 | bytes 12000000 | tf_op jit(solution)/shard_map/project_norm/pallas_call | solution.py:427
  131.8 1.0 copy.11
  132.8 1.0 copy.12
Async XLA Ops:
  0.6 1.1 copy-start.3
  1.7 1.1 copy-start.4
  2.8 1.1 copy-start.5
  3.8 1.1 copy-start.6
  4.9 123.0 %copy-start = (bf16[384,1536]{1,0:T(8,128)(2,1)S(1)}, bf16[384,1536]{1,0:T(8,128)(2,1)}, u32[]{:S(2)}) copy-start(bf16[384,1536]{1,0:T(8,128)(2,1)} %stream_ref.1) | copy-start | bytes 3538948
  4.9 123.0 %copy-start.1 = (f32[3072]{0:T(1024)S(1)}, f32[3072]{0:T(1024)}, u32[]{:S(2)}) copy-start(f32[3072]{0:T(1024)} %param.11) | copy-start | bytes 36868
  4.9 123.0 %copy-start.2 = (f32[3072]{0:T(1024)S(1)}, f32[3072]{0:T(1024)}, u32[]{:S(2)}) copy-start(f32[3072]{0:T(1024)} %param.12) | copy-start | bytes 36868

commit v3 on v2

--- a/solution.py
+++ b/solution.py
@@ -186,7 +186,8 @@
         start_own(0, c)
         return carry
 
-    lax.fori_loop(0, chunks, first_sends, 0)
+    ahead_of = min(2, chunks)
+    lax.fori_loop(0, ahead_of, first_sends, 0)
     for direction in (1, 0):
         if reach[direction] > 0:
             ring_copy(direction, 1, True).start()
@@ -252,18 +253,26 @@
                 attend_slot(span, 2, c)
             guarded(inner if has is True else inner & has, body)
 
-    def step(c, carry):
+    def near_blocks(c):
         arrived(0, 1, c)
         pass_straight(0, c)
-        pass_crossed(0, c)
         for span, has in valid[1:]:
             def body(span=span):
                 arrived(span, 0, c)
                 start_own(span, c)
             guarded(has, body)
+        pass_crossed(0, c)
+
+        @pl.when(c + ahead_of < chunks)
+        def _():
+            first_sends(c + ahead_of, 0)
+
+    def near_attend(c):
         attend_slot(0, 1, c)
         for span, has in valid[1:]:
             guarded(has, lambda span=span: attend_slot(span, 0, c))
+
+    def passed_blocks(c):
         for span, has in valid[1:]:
             def body(span=span):
                 arrived(span, 1, c)
@@ -271,19 +280,23 @@
                 pass_crossed(span, c)
                 attend_slot(span, 1, c)
             guarded(has, body)
-        pl.when(c > 0)(lambda: far_blocks(c - 1))
-        pl.when(c < reach[1])(lambda: weight_step(c + 1))
-        return carry
-
-    lax.fori_loop(0, chunks, step, 0)
+
+    def step(c, carry):
+        pl.when(c < chunks)(lambda: near_blocks(c))
+        pl.when((c >= 1) & (c <= chunks))(lambda: passed_blocks(c - 1))
+        pl.when(c < chunks)(lambda: near_attend(c))
+        pl.when(c >= 2)(lambda: far_blocks(c - 2))
+        pl.when((c >= 1) & (c <= reach[1]))(lambda: weight_step(c))
+        return carry
+
+    lax.fori_loop(0, chunks + 2, step, 0)
 
     def late_weights(c, carry):
         weight_step(c + 1)
         return carry
 
-    if reach[1] > chunks:
-        lax.fori_loop(chunks, reach[1], late_weights, 0)
-    far_blocks(chunks - 1)
+    if reach[1] > chunks + 1:
+        lax.fori_loop(chunks + 1, reach[1], late_weights, 0)
 
     for head in range(features // HD):
         done = acc[head] / total[head]

time: 136 us -> 113 us (0.83); the launches traced: 134 us -> 113 us
  Pallas kernels: 127 us -> 106 us
    pallas_call x1, Pallas kernels: 123 us -> 102 us  [attention(): pl.pallas_call(functools.partial(attention_kernel, layers, spans, chunk,...]
where the time goes in v3:
time: 113 us
  Pallas kernels  106 us (94%)
  local copies, waits for them, and re-layouts  6.29 us (6%)
    pallas_call x1, Pallas kernels, attention(): pl.pallas_call(functools.partial(attention_kernel, layers, spans, chunk,...  102 us
    unnamed x16, local copies, waits for them, and re-layouts  6.29 us
    pallas_call x1, Pallas kernels, project(): pl.pallas_call(functools.partial(project_kernel, width), out_shape=(jax.S...  3.85 us

profile of v3, /device:TPU:27, one launch (start us, length us, event | category | flops | bytes accessed | tf_op | source)
XLA Modules:
  0.0 113.1 jit_solution(2650636010970279178)
XLA Ops:
  0.6 0.0 copy-start.3
  0.6 1.1 copy-done.3
  1.7 0.0 copy-start.4
  1.7 1.1 copy-done.4
  2.8 0.0 copy-start.5
  2.8 1.1 copy-done.5
  3.8 0.0 copy-start.6
  3.8 1.1 copy-done.6
  4.9 0.0 copy-start
  4.9 0.0 copy-start.1
  4.9 0.0 copy-start.2
  4.9 102.3 %tile_attention.1 = (bf16[2,384,768]{2,1,0:T(8,128)(2,1)S(1)}, bf16[1536,1536]{1,0:T(8,128)(2,1)S(1)}) custom-call(bf16[384,768]{1,0:T(8,128)(2,1)S(1)} %copy-done.3, bf16[384,768]{1,0:T(8,128)(2,1)S(1)} %copy-done.4, bf16[384,768]{1,0:T(8,128)(2,1)S(1)} %copy-done.5, bf16[192,1536]{1,0:T(8,128)(2,1)S(1)} %copy-done.6), custom_call_target="tpu_custom_call" | custom-call | flops 2717908992 | bytes 100000000 | tf_op jit(solution)/shard_map/tile_attention/pallas_call | solution.py:347
  107.2 0.0 copy-done
  107.2 0.0 copy-done.1
  107.2 0.0 copy-done.2
  107.2 3.8 %project_norm.1 = (bf16[384,1536]{1,0:T(8,128)(2,1)S(1)}, bf16[384,1536]{1,0:T(8,128)(2,1)S(1)}) custom-call(bf16[2,384,768]{2,1,0:T(8,128)(2,1)S(1)} %get-tuple-element.4.att_ref, bf16[1536,1536]{1,0:T(8,128)(2,1)S(1)} %get-tuple-element.5.weight_ref, bf16[384,1536]{1,0:T(8,128)(2,1)S(1)} %copy-done, f32[1,3072]{1,0:T(1,128)S(1)} %bitcast.2, ...), custom_call_target="tpu_custom_call" | custom-call | flops 1811939328 | bytes 12000000 | tf_op jit(solution)/shard_map/project_norm/pallas_call | solution.py:440
  111.1 1.0 copy.11
  112.1 1.0 copy.12
Async XLA Ops:
  0.6 1.1 copy-start.3
  1.7 1.1 copy-start.4
  2.8 1.1 copy-start.5
  3.8 1.1 copy-start.6
  4.9 102.3 %copy-start = (bf16[384,1536]{1,0:T(8,128)(2,1)S(1)}, bf16[384,1536]{1,0:T(8,128)(2,1)}, u32[]{:S(2)}) copy-start(bf16[384,1536]{1,0:T(8,128)(2,1)} %stream_ref.1) | copy-start | bytes 3538948
  4.9 102.3 %copy-start.1 = (f32[3072]{0:T(1024)S(1)}, f32[3072]{0:T(1024)}, u32[]{:S(2)}) copy-start(f32[3072]{0:T(1024)} %param.11) | copy-start | bytes 36868
  4.9 102.3 %copy-start.2 = (f32[3072]{0:T(1024)S(1)}, f32[3072]{0:T(1024)}, u32[]{:S(2)}) copy-start(f32[3072]{0:T(1024)} %param.12) | copy-start | bytes 36868
